TPU v7x, 256 devices: a whole 4x4x8 slice. The times are simulated.
256 devices in a mesh: group: 2 (over z_hi), dp: 8 (over x, core), tensor: 16 (over z_lo, y).
Axes of the slice: x: 4, y: 4, z: 8 (z_hi: 2, z_lo: 4; z = z_hi * 4 + z_lo), core: 2. Of those that a mesh axis runs over, the one named last changes fastest.
Arguments:
- teacher_hidden: bfloat16 [4096, 8192], P(('group', 'dp'), 'tensor'), may hold values from -6 to 6
- teacher_gain: float32 [8192], P('tensor'), may hold values from 0.1 to 1.9
- project_weight: bfloat16 [8192, 3584], P('tensor'), may hold values from -0.0625 to 0.0625
- student_hidden: bfloat16 [4096, 3584], P(('group', 'dp', 'tensor')), may hold values from -6 to 6
- student_gain: float32 [3584], replicated, may hold values from 0.1 to 1.9
- gate_weight: bfloat16 [3584, 9472], P(('group', 'dp'), 'tensor'), may hold values from -0.09375 to 0.09375
- up_weight: bfloat16 [3584, 9472], P(('group', 'dp'), 'tensor'), may hold values from -0.09375 to 0.09375
- down_weight: bfloat16 [9472, 3584], P('tensor', ('group', 'dp')), may hold values from -0.0625 to 0.0625
- owner_map: int32 [256, 1], P(('group', 'dp')), may hold values from 0 to 15; in each aligned block of 16 rows (0 to 15, 16 to 31, ...) at most 2 rows name the same one
- token_ids: int32 [4096], P(('group', 'dp', 'tensor')), may hold values from 0 to 511
- token_counts: int32 [256], P(('group', 'dp')), may hold values from 1 to 16
- id_weight: float32 [512], replicated, may hold values from 0.25 to 4
Outputs:
- student_out: bfloat16 [16, 16, 32, 3584], P(('group', 'dp'), 'tensor')
- down_grad: float32 [3584, 9472], P(('group', 'dp'), 'tensor')
Inputs may be any that keep to these rules, and one draw needn't show every extreme that they name: `owner_map`: of the 16 episodes of one index of group and dp (aligned blocks of 16 rows), at most 2 have the same owner; owner o is index o of group and dp in mesh order.
All inputs are finite; a program needn't handle non-finite values.
Results may differ from a plain program's by a relative error of at most 0.02.
Values may be sent and summed in bfloat16 or wider, within the bound.
No kernel may reach another device: no remote copies, remote signals or barrier semaphores. Data moves between devices by JAX's collectives and lax.ppermute only.
A program may use at most 128 MiB of HBM per device.

v0:
```python
import math

import jax
import jax.numpy as jnp
from jax import lax
from jax.sharding import Mesh
from jax.sharding import PartitionSpec as P

DT = 8192
EP_LEN = 16
TENSOR = ("tensor_0", "tensor_1")
GROUP_DP_TENSOR = ("group", "dp", "tensor_0", "tensor_1")


EPSILON = 1e-06


def side_by_side(arrays, axis, split_dim, concat_dim, along):
    columns = [a.reshape(*a.shape[:along], -1) for a in arrays]
    both = jnp.concatenate(columns, axis=along)
    result, at, finished = (
        lax.all_to_all(both, axis, split_axis=split_dim, concat_axis=concat_dim, tiled=True),
        0,
        [],
    )
    for a, column in zip(arrays, columns):
        slab = result[..., at : at + column.shape[along]]
        finished.append(slab.reshape(*slab.shape[:along], *a.shape[along:]))
        at += column.shape[along]
    return tuple(finished)


def copy_for_each(array, axis):
    devices = lax.axis_size(axis)
    return lax.all_to_all(
        jnp.broadcast_to(array[None], (devices, *array.shape)), axis, 0, 0, tiled=True
    )


def of_everyone(array, axis):
    return copy_for_each(array, axis).sum(axis=0)


def joined_along(tiles, dim):
    tiles = jnp.moveaxis(tiles, 0, dim)
    shape = tiles.shape
    return tiles.reshape(*shape[:dim], shape[dim] * shape[dim + 1], *shape[dim + 2 :])


def all_blocks(array, axes, turns):
    tiles = array
    for k in turns:
        tiles = lax.all_gather(tiles, axes[k])
    done = turns[::-1]
    back = [done.index(k) for k in range(len(axes))]
    tiles = tiles.transpose(*back, *range(len(axes), tiles.ndim))
    return tiles.reshape(-1, *array.shape)


def gather_axes(array, axes, turns, dim):
    return joined_along(all_blocks(array, axes, turns), dim)


def sent_together(arrays, axis, dim, along):
    both = jnp.concatenate(arrays, axis=along)
    result, at, finished = (lax.all_gather(both, axis, axis=dim, tiled=True), 0, [])
    for a in arrays:
        finished.append(lax.slice_in_dim(result, at, at + a.shape[along], axis=along))
        at += a.shape[along]
    return tuple(finished)


def build_selector(owner_local, owners, capacity):
    owner_list = owner_local[:, 0]
    onehot = (owner_list[:, None] == jnp.arange(owners, dtype=jnp.int32)[None, :]).astype(jnp.int32)
    earlier = jnp.cumsum(onehot, axis=0) - onehot
    rank_list = jnp.sum(earlier * onehot, axis=1)
    target = owner_list * capacity + rank_list
    return (target[None, :] == jnp.arange(owners * capacity, dtype=jnp.int32)[:, None]).astype(
        jnp.bfloat16
    )


def dispatch_rows(selector, values):
    return jnp.einsum("re,pef->prf", selector, values, preferred_element_type=jnp.float32).astype(
        jnp.bfloat16
    )


def dispatch_plain(selector, values):
    return jnp.einsum("re,pe->pr", selector, values, preferred_element_type=jnp.float32).astype(
        jnp.bfloat16
    )


def regroup_rows(payload):
    return (
        lax.all_to_all(payload[0], ("group", "dp"), split_axis=1, concat_axis=1, tiled=True),
        *side_by_side((payload[1], payload[2]), ("group", "dp"), 1, 1, 2),
    )


def teacher_scaling(raw_rows, teacher_gain):
    widened = raw_rows.astype(jnp.float32)
    return (
        jnp.sum(widened * widened, axis=1),
        (widened * teacher_gain[None, :]).astype(jnp.bfloat16),
    )


def local(
    teacher_hidden,
    teacher_gain,
    project_weight,
    student_hidden,
    student_gain,
    gate_weight,
    up_weight,
    down_weight,
    owner_map,
    token_ids,
    token_counts,
    id_weight,
):
    groups = lax.axis_size("group")
    places = lax.axis_size("dp")
    owners = groups * places
    tensors = lax.axis_size(TENSOR)
    tensor_index = lax.axis_index(TENSOR)
    episodes = token_counts.shape[0]
    own_span = EP_LEN // tensors
    capacity = max(2, 2 * episodes // owners)
    received = owners * capacity
    student_width = student_hidden.shape[1]
    selector = build_selector(owner_map, owners, capacity)
    id_rows = token_ids.reshape(own_span, episodes)
    looked = jnp.sum(
        jnp.where(
            id_rows[:, :, None] == jnp.arange(id_weight.shape[0], dtype=jnp.int32)[None, None, :],
            id_weight[None, None, :],
            0.0,
        ),
        axis=2,
    )
    position = tensor_index * own_span + jnp.arange(own_span, dtype=jnp.int32)[:, None]
    token_weight = jnp.where(position < token_counts[None, :], looked, 0.0).astype(jnp.bfloat16)
    sent_weight = dispatch_plain(selector, token_weight)
    sent_student = dispatch_rows(
        selector, student_hidden.reshape(own_span, episodes, student_width)
    )
    sent_raw = dispatch_rows(selector, teacher_hidden.reshape(EP_LEN, episodes, -1))
    arrived = regroup_rows((sent_raw, sent_student, sent_weight))
    squares, scaled = teacher_scaling(arrived[0].reshape(EP_LEN * received, -1), teacher_gain)
    totals = of_everyone(squares, TENSOR)
    inverse = lax.rsqrt(totals / DT + EPSILON)
    share_rows = own_span * received
    summed = lax.psum_scatter(
        jnp.dot(scaled, project_weight, preferred_element_type=jnp.float32).astype(jnp.bfloat16),
        TENSOR,
        scatter_dimension=0,
        tiled=True,
    ).astype(jnp.float32)
    own_inverse = lax.dynamic_slice_in_dim(inverse, tensor_index * share_rows, share_rows, 0)
    teacher_mine = (
        (summed * own_inverse[:, None])
        .astype(jnp.bfloat16)
        .reshape(own_span, received, student_width)
    )
    student_block = arrived[1].reshape(own_span * received, student_width).astype(jnp.float32)
    rescale = lax.rsqrt(jnp.mean(student_block * student_block, axis=1, keepdims=True) + EPSILON)
    normed = (student_block * rescale * student_gain[None, :]).astype(jnp.bfloat16)
    gathered = gather_axes(normed, TENSOR, (0, 1), 0)
    pieces = sent_together((gate_weight, up_weight), ("group", "dp"), 0, 1)
    gate_sum = jnp.dot(gathered, pieces[0], preferred_element_type=jnp.float32)
    up_sum = jnp.dot(gathered, pieces[1], preferred_element_type=jnp.float32)
    activated = (jax.nn.silu(gate_sum) * up_sum).astype(jnp.bfloat16)
    branch = jnp.dot(
        activated,
        lax.all_gather(down_weight, ("group", "dp"), axis=1, tiled=True),
        preferred_element_type=jnp.float32,
    )
    branch_local = lax.psum_scatter(
        branch.astype(jnp.bfloat16), TENSOR, scatter_dimension=0, tiled=True
    ).astype(jnp.float32)
    predicted = student_block + branch_local
    student_out = predicted.astype(jnp.bfloat16).reshape(1, own_span, received, student_width)
    difference = predicted - teacher_mine.reshape(-1, student_width).astype(jnp.float32)
    weight_rows = arrived[2].reshape(-1, 1).astype(jnp.float32)
    tokens_all = EP_LEN * episodes * owners
    grad_block = (weight_rows * difference * (1.0 / math.sqrt(tokens_all))).astype(jnp.bfloat16)
    grad_all = gather_axes(grad_block, TENSOR, (0, 1), 0)
    down_grad = lax.psum_scatter(
        jnp.einsum("rc,rh->ch", grad_all, activated, preferred_element_type=jnp.float32).astype(
            jnp.bfloat16
        ),
        ("group", "dp"),
        scatter_dimension=0,
        tiled=True,
    ).astype(jnp.float32)
    return (student_out, down_grad)


def solution(mesh):
    split = Mesh(
        mesh.devices.reshape(mesh.shape["group"], mesh.shape["dp"], 4, 4),
        ("group", "dp", "tensor_0", "tensor_1"),
    )
    placed = (
        P(("group", "dp"), TENSOR),
        P(TENSOR),
        P(TENSOR, None),
        P(GROUP_DP_TENSOR, None),
        P(),
        P(("group", "dp"), TENSOR),
        P(("group", "dp"), TENSOR),
        P(TENSOR, ("group", "dp")),
        P(("group", "dp"), None),
        P(GROUP_DP_TENSOR),
        P(("group", "dp")),
        P(),
    )
    return jax.shard_map(
        local,
        mesh=split,
        in_specs=placed,
        out_specs=(P(("group", "dp"), TENSOR, None, None), P(("group", "dp"), TENSOR)),
        check_vma=False,
    )
```

profile of v0, /device:TPU:32, one launch (start us, length us, event | category | flops | bytes accessed | tf_op | source)
XLA Modules:
  0.0 587.0 jit_solution(2817465092216490723)
XLA Ops:
  12.2 1.2 fusion.4
  14.3 2.1 reduce.5
  16.5 24.2 %all_to_all.16 = bf16[16,2,3585]{2,1,0:T(2,128)(2,1)S(1)} all-to-all(bf16[16,2,3585]{2,1,0:T(2,128)(2,1)S(1)} %reshape.162), channel_id=1, replica_groups=mesh['group'=2,'dp'=8,'tensor_0'=4,'tensor_1'=4] {'group','dp'}, dimensions={0} | all-to-all | bytes 458880 | tf_op jit(solution)/shard_map/all_to_all | solution.py:22
  41.7 17.8 %all_gather.28 = bf16[4,32,3584]{2,1,0:T(8,128)(2,1)} all-gather(bf16[1,32,3584]{2,1,0:T(8,128)(2,1)S(1)} %fusion.19), channel_id=1, replica_groups=mesh['group'=2,'dp'=8,'tensor_0'=4,'tensor_1'=4] {'tensor_0'}, dimensions={0}, use_global_device_ids=true | all-gather | bytes 1146880 | tf_op jit(solution)/shard_map/all_gather | solution.py:53
  62.1 23.2 %all_to_all.17 = bf16[16,32,512]{2,0,1:T(8,128)(2,1)S(1)} all-to-all(bf16[16,32,512]{2,0,1:T(8,128)(2,1)S(1)} %copy.43), channel_id=1, replica_groups=mesh['group'=2,'dp'=8,'tensor_0'=4,'tensor_1'=4] {'group','dp'}, dimensions={1} | all-to-all | bytes 1048576 | tf_op jit(solution)/shard_map/all_to_all | solution.py:98
  85.8 3.9 convolution_convert_fusion.1
  89.9 16.8 %all-gather.12.cloned.1.call-done = bf16[16,32,3584]{2,1,0:T(8,128)(2,1)} async-done(((bf16[4,32,3584]{2,1,0:T(8,128)(2,1)}), bf16[16,32,3584]{2,1,0:T(8,128)(2,1)}) %all-gather.12.cloned.1.call-update) | async-done | bytes 3670032 | tf_op jit(solution)/shard_map/all_gather | solution.py:53
  106.7 4.2 copy.42
  110.8 115.0 %all-gather.8.cloned.1.call-done = bf16[3584,1184]{1,0:T(8,128)(2,1)} async-done(((bf16[224,1184]{1,0:T(8,128)(2,1)}), bf16[3584,1184]{1,0:T(8,128)(2,1)}) %all-gather.8.cloned.1.call-update) | async-done | bytes 8486928 | tf_op jit(solution)/shard_map/all_gather | solution.py:66
  225.8 5.9 %fusion.2 = f32[512,592]{0,1:T(8,128)S(1)} fusion(bf16[512,3584]{1,0:T(8,128)(2,1)} %bitcast.71, bf16[3584,1184]{1,0:T(8,128)(2,1)} %all-gather.8.cloned.1.call-done), kind=kOutput, calls=%fused_computation.5 | convolution fusion | flops 2172649472 | bytes 9469952 | tf_op jit(solution)/shard_map/dot_general | solution.py:174
  231.8 1.2 copy-done.6
  232.9 4.2 fusion.8
  237.2 68.6 %all-gather.10.cloned.1.call-done = bf16[592,3584]{0,1:T(8,128)(2,1)} async-done(((bf16[592,224]{0,1:T(8,128)(2,1)}), bf16[592,3584]{0,1:T(8,128)(2,1)}) %all-gather.10.cloned.1.call-update) | async-done | bytes 4243472 | tf_op jit(solution)/shard_map/all_gather | solution.py:179
  305.7 6.9 %convolution_convert_fusion.2 = bf16[512,3584]{1,0:T(8,128)(2,1)} fusion(bf16[512,592]{0,1:T(8,128)(2,1)S(1)} %fusion.8, bf16[592,3584]{0,1:T(8,128)(2,1)} %all-gather.10.cloned.1.call-done), kind=kOutput, calls=%fused_computation.2 | convolution fusion | flops 2174484480 | bytes 8519680 | tf_op jit(solution)/shard_map/dot_general | solution.py:177
  313.7 5.8 all-to-all-start.2
  319.8 6.4 %all-to-all-done.2 = f32[16,1,512]{2,1,0:T(1,128)S(1)} async-done(((f32[16,1,512]{2,1,0:T(1,128)}), f32[16,1,512]{2,1,0:T(1,128)S(1)}, u32[]{:S(2)}, u32[]{:S(2)}) %all-to-all-start.2) | async-done | bytes 32800 | tf_op jit(solution)/shard_map/all_to_all | solution.py:35
  326.3 68.7 %reduce-scatter.4.cloned.1.call-done = bf16[32,3584]{1,0:T(8,128)(2,1)} async-done(((bf16[512,3584]{1,0:T(8,128)(2,1)}), bf16[32,3584]{1,0:T(8,128)(2,1)}) %reduce-scatter.4.cloned.1.call-update) | async-done | bytes 229392 | tf_op jit(solution)/shard_map/reduce_scatter | solution.py:182
  395.0 1.9 multiply_convert_fusion
  396.9 20.9 %all-gather.1 = bf16[128,3584]{1,0:T(8,128)(2,1)} all-gather(bf16[32,3584]{1,0:T(8,128)(2,1)S(1)} %get-tuple-element.4), channel_id=3, replica_groups=mesh['group'=2,'dp'=8,'tensor_0'=4,'tensor_1'=4] {'tensor_0'}, dimensions={0}, use_global_device_ids=true | all-gather | bytes 1146880 | tf_op jit(solution)/shard_map/all_gather | solution.py:53
  417.9 46.3 %all-gather.14.cloned.1.call-done = bf16[16,32,3584]{2,1,0:T(8,128)(2,1)} async-done(((bf16[4,32,3584]{2,1,0:T(8,128)(2,1)}), bf16[16,32,3584]{2,1,0:T(8,128)(2,1)}) %all-gather.14.cloned.1.call-update) | async-done | bytes 3670032 | tf_op jit(solution)/shard_map/all_gather | solution.py:53
  464.2 2.3 copy.46
  466.5 4.7 convolution_convert_fusion
  471.2 106.9 %reduce-scatter.8.cloned.1.call-done = bf16[224,592]{1,0:T(8,128)(2,1)} async-done(((bf16[3584,592]{1,0:T(8,128)(2,1)}), bf16[224,592]{1,0:T(8,128)(2,1)}) %reduce-scatter.8.cloned.1.call-update) | async-done | bytes 265232 | tf_op jit(solution)/shard_map/reduce_scatter | solution.py:192
  578.1 1.8 convert_element_type.128
  (58 shorter events, 11.0 us)
Async XLA Ops:
  8.0 53.4 %copy-start = (bf16[256,512]{1,0:T(8,128)(2,1)S(1)}, bf16[256,512]{1,0:T(8,128)(2,1)}, u32[]{:S(2)}) copy-start(bf16[256,512]{1,0:T(8,128)(2,1)} %param.12) | copy-start | bytes 786436
  8.0 33.6 %copy-start.4 = (f32[3584]{0:T(1024)S(1)}, f32[3584]{0:T(1024)}, u32[]{:S(2)}) copy-start(f32[3584]{0:T(1024)} %param.16) | copy-start | bytes 43012
  8.0 98.6 %all-gather.12.cloned.1.call-start = ((), (), s32[]{:S(2)}) async-start(), calls=%async_computation.11 | async-start | bytes 4587520 | tf_op jit(solution)/shard_map/all_gather | solution.py:53
  13.4 46.2 %copy-start.2 = (bf16[224,592]{1,0:T(8,128)(2,1)S(1)}, bf16[224,592]{1,0:T(8,128)(2,1)}, u32[]{:S(2)}) copy-start(bf16[224,592]{1,0:T(8,128)(2,1)} %param.18) | copy-start | bytes 795652
  13.4 46.2 %copy-start.3 = (bf16[224,592]{1,0:T(8,128)(2,1)S(1)}, bf16[224,592]{1,0:T(8,128)(2,1)}, u32[]{:S(2)}) copy-start(bf16[224,592]{1,0:T(8,128)(2,1)} %param.17) | copy-start | bytes 795652
  59.5 26.1 %copy-start.5 = (f32[512]{0:T(512)S(1)}, f32[512]{0:T(512)}, u32[]{:S(2)}) copy-start(f32[512]{0:T(512)} %param.13) | copy-start | bytes 6148
  59.6 166.2 %all-gather.8.cloned.1.call-start = ((), (), s32[]{:S(2)}) async-start(), calls=%async_computation.6 | async-start | bytes 9748480 | tf_op jit(solution)/shard_map/all_gather | solution.py:66
  60.6 245.1 %all-gather.10.cloned.1.call-start = ((), (), s32[]{:S(2)}) async-start(), calls=%async_computation.7 | async-start | bytes 4874240 | tf_op jit(solution)/shard_map/all_gather | solution.py:179
  61.4 265.0 %reduce-scatter.6.cloned.1.call-start = ((), (), s32[]{:S(2)}) async-start(), calls=%async_computation.9 | async-start | bytes 3899392 | tf_op jit(solution)/shard_map/reduce_scatter | solution.py:157
  61.4 24.3 %copy-start.7 = (bf16[512,3584]{1,0:T(8,128)(2,1)S(1)}, bf16[512,3584]{1,0:T(8,128)(2,1)}, u32[]{:S(2)}) copy-start(bf16[512,3584]{1,0:T(8,128)(2,1)} %param.14) | copy-start | bytes 11010052
  89.7 305.3 %reduce-scatter.4.cloned.1.call-start = ((), (), s32[]{:S(2)}) async-start(), calls=%async_computation.8 | async-start | bytes 3899392 | tf_op jit(solution)/shard_map/reduce_scatter | solution.py:182
  225.8 6.0 %copy-start.1 = (bf16[4,4,32,3584]{3,2,1,0:T(8,128)(2,1)S(1)}, bf16[4,4,32,3584]{3,2,1,0:T(8,128)(2,1)}, u32[]{:S(2)}) copy-start(bf16[4,4,32,3584]{3,2,1,0:T(8,128)(2,1)} %copy.42) | copy-start | bytes 11010052
  225.8 7.1 %copy-start.6 = (bf16[3584,1184]{1,0:T(8,128)(2,1)S(1)}, bf16[3584,1184]{1,0:T(8,128)(2,1)}, u32[]{:S(2)}) copy-start(bf16[3584,1184]{1,0:T(8,128)(2,1)} %all-gather.8.cloned.1.call-done) | copy-start | bytes 25460740
  313.7 12.5 %all-to-all-start.2 = ((f32[16,1,512]{2,1,0:T(1,128)}), f32[16,1,512]{2,1,0:T(1,128)S(1)}, u32[]{:S(2)}, u32[]{:S(2)}) async-start(f32[16,1,512]{2,1,0:T(1,128)} %broadcast_in_dim.38), calls=%async_computation.4 | async-start | bytes 65536 | tf_op jit(solution)/shard_map/all_to_all | solution.py:35
  319.5 144.7 %all-gather.14.cloned.1.call-start = ((), (), s32[]{:S(2)}) async-start(), calls=%async_computation.12 | async-start | bytes 4587520 | tf_op jit(solution)/shard_map/all_gather | solution.py:53
  417.8 160.3 %reduce-scatter.8.cloned.1.call-start = ((), (), s32[]{:S(2)}) async-start(), calls=%async_computation.10 | async-start | bytes 4874240 | tf_op jit(solution)/shard_map/reduce_scatter | solution.py:192
Sparse Core Ops, SparseCore 0:
  59.7 46.9 all-gather.11
  109.9 115.8 all-gather.7
  228.5 77.1 all-gather.9
  417.9 46.2 all-gather.13
  471.3 106.7 reduce-scatter.7
Sparse Core Ops, SparseCore 1:
  89.7 134.8 reduce-scatter.5
  312.7 82.2 reduce-scatter.3
where the time goes:
time: 589 us; the launch traced here: 587 us
  waiting for transfers between devices  429 us (73%)
  blocking collectives  86 us (15%)
  matrix products  28.1 us (5%)
  between operations  15.4 us (3%)
  other arithmetic  11.4 us (2%)
  local copies, waits for them, and re-layouts  10.5 us (2%)
  starting transfers between devices  6.23 us (1%)
    all_gather x1, waiting for transfers between devices, sent_together(): lax.all_gather(both, axis, axis=dim, tiled=True)  115 us
    reduce_scatter x1, waiting for transfers between devices, local(): lax.psum_scatter(jnp.einsum('rc,rh->ch', grad_all, activated, preferred_e...  107 us
    reduce_scatter x1, waiting for transfers between devices, local(): lax.psum_scatter(branch.astype(jnp.bfloat16), TENSOR, scatter_dimension=0...  68.7 us
    all_gather x1, waiting for transfers between devices, local(): lax.all_gather(down_weight, ('group', 'dp'), axis=1, tiled=True)  68.6 us
    all_gather x2, waiting for transfers between devices, all_blocks(): tiles = lax.all_gather(tiles, axes[k])  63.1 us
    all_gather x2, blocking collectives, all_blocks(): tiles = lax.all_gather(tiles, axes[k])  38.7 us
    all_to_all x1, blocking collectives, side_by_side(): lax.all_to_all(both, axis, split_axis=split_dim, concat_axis=concat_dim,...  24.2 us
    all_to_all x1, blocking collectives, regroup_rows(): lax.all_to_all(payload[0], ('group', 'dp'), split_axis=1, concat_axis=1,...  23.2 us
  transfers between devices with their start and end apart: 8, of which 7 were waited for; matrix products, arithmetic and copies ran while one was open for 5% of the time, Pallas kernels for 0%

commit v1 on v0

v1 whole, which is shorter than its diff:
```python
import math

import jax
import jax.numpy as jnp
from jax import lax
from jax.sharding import Mesh
from jax.sharding import PartitionSpec as P

DT = 8192
EP_LEN = 16
TENSOR = ("tensor_0", "tensor_1")
OWNERS = ("group", "dp")
GROUP_DP_TENSOR = ("group", "dp", "tensor_0", "tensor_1")
EPSILON = 1e-06


def build_selector(owner_local, owners, capacity):
    owner = owner_local[:, 0]
    index = jnp.arange(owner.shape[0], dtype=jnp.int32)
    earlier = (owner[None, :] == owner[:, None]) & (index[None, :] < index[:, None])
    target = owner * capacity + jnp.sum(earlier.astype(jnp.int32), axis=1)
    slots = jnp.arange(owners * capacity, dtype=jnp.int32)
    return (target[None, :] == slots[:, None]).astype(jnp.bfloat16)


def local(
    teacher_hidden,
    teacher_gain,
    project_weight,
    student_hidden,
    student_gain,
    gate_weight,
    up_weight,
    down_weight,
    owner_map,
    token_ids,
    token_counts,
    id_weight,
):
    owners = lax.axis_size(OWNERS)
    episodes = token_counts.shape[0]
    capacity = max(2, 2 * episodes // owners)
    hidden = gate_weight.shape[1]
    position = lax.axis_index(TENSOR)
    tokens_all = EP_LEN * episodes * owners

    student = student_hidden.astype(jnp.float32)
    rescale = lax.rsqrt(jnp.mean(student * student, axis=1, keepdims=True) + EPSILON)
    normed = (student * rescale * student_gain[None, :]).astype(jnp.bfloat16)
    gathered = lax.all_gather(normed, TENSOR, axis=0, tiled=True)

    both = lax.all_gather(
        jnp.concatenate([gate_weight, up_weight], axis=1), OWNERS, axis=0, tiled=True
    )
    down = lax.all_gather(down_weight, OWNERS, axis=1, tiled=True)

    widened = teacher_hidden.astype(jnp.float32)
    squares = jnp.sum(widened * widened, axis=1)
    scaled = (widened * teacher_gain[None, :]).astype(jnp.bfloat16)
    totals = lax.psum_scatter(squares, TENSOR, scatter_dimension=0, tiled=True)
    inverse = lax.rsqrt(totals / DT + EPSILON)
    summed = lax.psum_scatter(
        jnp.dot(scaled, project_weight, preferred_element_type=jnp.float32).astype(jnp.bfloat16),
        TENSOR,
        scatter_dimension=0,
        tiled=True,
    ).astype(jnp.float32)
    projected = (summed * inverse[:, None]).astype(jnp.bfloat16).astype(jnp.float32)

    sums = jnp.dot(gathered, both, preferred_element_type=jnp.float32)
    activated = (jax.nn.silu(sums[:, :hidden]) * sums[:, hidden:]).astype(jnp.bfloat16)
    branch = jnp.dot(activated, down, preferred_element_type=jnp.float32).astype(jnp.bfloat16)
    branch_local = lax.psum_scatter(branch, TENSOR, scatter_dimension=0, tiled=True)
    predicted = student + branch_local.astype(jnp.float32)

    ids = jnp.arange(id_weight.shape[0], dtype=jnp.int32)
    looked = jnp.sum(jnp.where(token_ids[:, None] == ids[None, :], id_weight[None, :], 0.0), axis=1)
    weight = jnp.where(position < token_counts, looked, 0.0).astype(jnp.bfloat16)
    scale = 1.0 / math.sqrt(tokens_all)
    grad = (weight.astype(jnp.float32)[:, None] * (predicted - projected) * scale).astype(
        jnp.bfloat16
    )
    grad_all = lax.all_gather(grad, TENSOR, axis=0, tiled=True)
    down_grad = lax.psum_scatter(
        jnp.einsum("rc,rh->ch", grad_all, activated, preferred_element_type=jnp.float32).astype(
            jnp.bfloat16
        ),
        OWNERS,
        scatter_dimension=0,
        tiled=True,
    ).astype(jnp.float32)

    selector = build_selector(owner_map, owners, capacity)
    sent = jnp.dot(
        selector, predicted.astype(jnp.bfloat16), preferred_element_type=jnp.float32
    ).astype(jnp.bfloat16)
    student_out = lax.all_to_all(sent, OWNERS, 0, 0, tiled=True)
    return (student_out[None, None], down_grad)


def solution(mesh):
    split = Mesh(
        mesh.devices.reshape(mesh.shape["group"], mesh.shape["dp"], 4, 4),
        ("group", "dp", "tensor_0", "tensor_1"),
    )
    placed = (
        P(OWNERS, TENSOR),
        P(TENSOR),
        P(TENSOR, None),
        P(GROUP_DP_TENSOR, None),
        P(),
        P(OWNERS, TENSOR),
        P(OWNERS, TENSOR),
        P(TENSOR, OWNERS),
        P(OWNERS, None),
        P(GROUP_DP_TENSOR),
        P(OWNERS),
        P(),
    )
    return jax.shard_map(
        local,
        mesh=split,
        in_specs=placed,
        out_specs=(P(OWNERS, TENSOR, None, None), P(OWNERS, TENSOR)),
        check_vma=False,
    )
```

time: 589 us -> 662 us (1.12)
  waiting for transfers between devices: 429 us -> 555 us
  blocking collectives: 86 us -> 56.2 us
  local copies, waits for them, and re-layouts: 10.5 us -> 2.74 us
    all_gather x4, waiting for transfers between devices: 247 us -> 342 us  [the longest x1 122 us: local(): lax.all_gather(jnp.concatenate([gate_weight, up_weight], axis=1), OWNERS,...]
    all_gather x2 -> x0, blocking collectives: 38.7 us -> none  [all_blocks(): tiles = lax.all_gather(tiles, axes[k])]
    reduce_scatter x1, waiting for transfers between devices: 0.01 us -> 37.6 us  [local(): lax.psum_scatter(jnp.dot(scaled, project_weight, preferred_element_type=j...]
    unnamed x0 -> x1, blocking collectives: none -> 34.1 us
    all_to_all x2 -> x1, blocking collectives: 47.3 us -> 22.1 us  [local(): student_out = lax.all_to_all(sent, OWNERS, 0, 0, tiled=True)]
    reduce_scatter x1, waiting for transfers between devices: 107 us -> 87.8 us  [local(): lax.psum_scatter(jnp.einsum('rc,rh->ch', grad_all, activated, preferred_e...]
    reduce_scatter x1, waiting for transfers between devices: 68.7 us -> 86.1 us  [local(): lax.psum_scatter(branch, TENSOR, scatter_dimension=0, tiled=True)]
    dot_general x6 -> x3, matrix products: 19.5 us -> 13.2 us  [the longest x1 7.77 us: local(): sums = jnp.dot(gathered, both, preferred_element_type=jnp.float32)]
  transfers between devices with their start and end apart: 8 -> 7, of which waited for: 7 -> 7; matrix products, arithmetic and copies ran while one was open for 5% -> 3% of each run, Pallas kernels for 0% -> 0%
where the time goes in v1:
time: 662 us; the launch traced here: 661 us
  waiting for transfers between devices  555 us (84%)
  blocking collectives  56.2 us (8%)
  matrix products  22.8 us (3%)
  between operations  14.9 us (2%)
  other arithmetic  9.05 us (1%)
    all_gather x1, waiting for transfers between devices, local(): lax.all_gather(jnp.concatenate([gate_weight, up_weight], axis=1), OWNERS,...  122 us
    reduce_scatter x1, waiting for transfers between devices, local(): lax.psum_scatter(jnp.einsum('rc,rh->ch', grad_all, activated, preferred_e...  87.8 us
    reduce_scatter x1, waiting for transfers between devices, local(): lax.psum_scatter(branch, TENSOR, scatter_dimension=0, tiled=True)  86.1 us
    all_gather x1, waiting for transfers between devices, local(): grad_all = lax.all_gather(grad, TENSOR, axis=0, tiled=True)  79.6 us
    all_gather x1, waiting for transfers between devices, local(): gathered = lax.all_gather(normed, TENSOR, axis=0, tiled=True)  71.6 us
    all_gather x1, waiting for transfers between devices, local(): down = lax.all_gather(down_weight, OWNERS, axis=1, tiled=True)  69.5 us
    reduce_scatter x1, waiting for transfers between devices, local(): lax.psum_scatter(jnp.dot(scaled, project_weight, preferred_element_type=j...  37.6 us
    unnamed x1, blocking collectives  34.1 us
  transfers between devices with their start and end apart: 7, of which 7 were waited for; matrix products, arithmetic and copies ran while one was open for 3% of the time, Pallas kernels for 0%

profile of v1, /device:TPU:32, one launch (start us, length us, event | category | flops | bytes accessed | tf_op | source)
XLA Modules:
  0.0 660.6 jit_solution(17144854641354540357)
XLA Ops:
  7.2 1.1 fusion.5
  8.3 1.6 fusion.7
  10.0 2.0 pad_maximum_fusion
  12.1 0.7 all-gather.9.cloned.1.call-update
  12.9 4.4 convolution_convert_fusion.2
  17.3 71.6 %all-gather.5.cloned.1.call-done = bf16[256,3584]{1,0:T(8,128)(2,1)} async-done(((bf16[16,3584]{1,0:T(8,128)(2,1)}), bf16[256,3584]{1,0:T(8,128)(2,1)}) %all-gather.5.cloned.1.call-update) | async-done | bytes 1835024 | tf_op jit(solution)/shard_map/all_gather | solution.py:50
  88.9 121.7 %all-gather.7.cloned.1.call-done = bf16[3584,1184]{1,0:T(8,128)(2,1)} async-done(((bf16[224,1184]{1,0:T(8,128)(2,1)}), bf16[3584,1184]{1,0:T(8,128)(2,1)}) %all-gather.7.cloned.1.call-update) | async-done | bytes 8486928 | tf_op jit(solution)/shard_map/all_gather | solution.py:52
  210.6 7.8 %fusion.16 = f32[256,1184]{0,1:T(8,128)S(1)} fusion(bf16[256,3584]{1,0:T(8,128)(2,1)} %all-gather.5.cloned.1.call-done, bf16[3584,1184]{1,0:T(8,128)(2,1)} %all-gather.7.cloned.1.call-done), kind=kOutput, calls=%fused_computation.36 | convolution fusion | flops 2172649472 | bytes 11534336 | tf_op jit(solution)/shard_map/dot_general | solution.py:70
  218.6 69.5 %all-gather.9.cloned.1.call-done = bf16[592,3584]{0,1:T(8,128)(2,1)} async-done(((bf16[592,224]{0,1:T(8,128)(2,1)}), bf16[592,3584]{0,1:T(8,128)(2,1)}) %all-gather.9.cloned.1.call-update) | async-done | bytes 4243472 | tf_op jit(solution)/shard_map/all_gather | solution.py:55
  288.0 5.2 convolution_convert_fusion.1
  293.4 0.6 copy-done.8
  293.9 0.6 dynamic-slice
  295.3 34.1 %all-reduce = f32[256]{0:T(256)S(1)} all-reduce(f32[256]{0:T(256)S(1)} %fusion.2), channel_id=4, replica_groups=mesh['group'=2,'dp'=8,'tensor_0'=4,'tensor_1'=4] {'tensor_0','tensor_1'}, use_global_device_ids=true, to_apply=%region_6.7.clone | all-reduce | flops 256 | bytes 2048
  329.7 37.6 %reduce-scatter.6.cloned.1.call-done = bf16[16,3584]{1,0:T(8,128)(2,1)} async-done(((bf16[256,3584]{1,0:T(8,128)(2,1)}), bf16[16,3584]{1,0:T(8,128)(2,1)}) %reduce-scatter.6.cloned.1.call-update) | async-done | bytes 114704 | tf_op jit(solution)/shard_map/reduce_scatter | solution.py:62
  367.3 86.1 %reduce-scatter.4.cloned.1.call-done = bf16[16,3584]{1,0:T(8,128)(2,1)} async-done(((bf16[256,3584]{1,0:T(8,128)(2,1)}), bf16[16,3584]{1,0:T(8,128)(2,1)}) %reduce-scatter.4.cloned.1.call-update) | async-done | bytes 114704 | tf_op jit(solution)/shard_map/reduce_scatter | solution.py:73
  453.4 1.7 multiply_convert_fusion
  455.2 79.6 %all-gather.11.cloned.1.call-done = bf16[256,3584]{1,0:T(8,128)(2,1)} async-done(((bf16[16,3584]{1,0:T(8,128)(2,1)}), bf16[256,3584]{1,0:T(8,128)(2,1)}) %all-gather.11.cloned.1.call-update) | async-done | bytes 1835024 | tf_op jit(solution)/shard_map/all_gather | solution.py:83
  534.8 5.2 convolution_convert_fusion
  540.0 0.6 copy-done.7
  540.9 0.2 convolution_convert_fusion.3
  541.2 22.1 %all_to_all.9 = bf16[16,2,3584]{2,1,0:T(2,128)(2,1)S(1)} all-to-all(bf16[16,2,3584]{2,1,0:T(2,128)(2,1)S(1)} %all_to_all.6), channel_id=1, replica_groups=mesh['group'=2,'dp'=8,'tensor_0'=4,'tensor_1'=4] {'group','dp'}, dimensions={0} | all-to-all | bytes 458752 | tf_op jit(solution)/shard_map/all_to_all | solution.py:97
  563.3 0.8 broadcast_in_dim.18
  564.1 87.8 %reduce-scatter.8.cloned.1.call-done = bf16[224,592]{1,0:T(8,128)(2,1)} async-done(((bf16[3584,592]{1,0:T(8,128)(2,1)}), bf16[224,592]{1,0:T(8,128)(2,1)}) %reduce-scatter.8.cloned.1.call-update) | async-done | bytes 265232 | tf_op jit(solution)/shard_map/reduce_scatter | solution.py:84
  651.9 1.8 convert_element_type.76
  (38 shorter events, 1.4 us)
Async XLA Ops:
  7.2 5.7 copy-start.1
  7.2 5.7 copy-start.3
  7.2 81.7 %all-gather.5.cloned.1.call-start = ((), (), s32[]{:S(2)}) async-start(), calls=%async_computation.4 | async-start | bytes 1949696 | tf_op jit(solution)/shard_map/all_gather | solution.py:50
  10.0 200.6 %all-gather.7.cloned.1.call-start = ((), (), s32[]{:S(2)}) async-start(), calls=%async_computation.5 | async-start | bytes 9748480 | tf_op jit(solution)/shard_map/all_gather | solution.py:52
  12.1 276.0 %all-gather.9.cloned.1.call-start = ((), (), s32[]{:S(2)}) async-start(), calls=%async_computation.6 | async-start | bytes 4874240 | tf_op jit(solution)/shard_map/all_gather | solution.py:55
  12.8 354.5 %reduce-scatter.6.cloned.1.call-start = ((), (), s32[]{:S(2)}) async-start(), calls=%async_computation.8 | async-start | bytes 1949696 | tf_op jit(solution)/shard_map/reduce_scatter | solution.py:62
  17.3 436.1 %reduce-scatter.4.cloned.1.call-start = ((), (), s32[]{:S(2)}) async-start(), calls=%async_computation.7 | async-start | bytes 1949696 | tf_op jit(solution)/shard_map/reduce_scatter | solution.py:73
  293.2 0.7 copy-start.8
  293.2 36.2 %copy-start.4 = (f32[512]{0:T(512)S(1)}, f32[512]{0:T(512)}, u32[]{:S(2)}) copy-start(f32[512]{0:T(512)} %param.23) | copy-start | bytes 6148
  293.3 36.2 %copy-start.5 = (s32[16]{0:T(128)S(1)}, s32[16]{0:T(128)}, u32[]{:S(2)}) copy-start(s32[16]{0:T(128)} %param.21) | copy-start | bytes 196
  293.3 36.4 %copy-start.6 = (s32[16]{0:T(128)S(1)}, s32[16]{0:T(128)}, u32[]{:S(2)}) copy-start(s32[16]{0:T(128)} %param.22) | copy-start | bytes 196
  293.3 160.2 %copy-start = (bf16[16,3584]{1,0:T(8,128)(2,1)S(1)}, bf16[16,3584]{1,0:T(8,128)(2,1)}, u32[]{:S(2)}) copy-start(bf16[16,3584]{1,0:T(8,128)(2,1)} %param.15) | copy-start | bytes 344068
  293.3 241.5 %all-gather.11.cloned.1.call-start = ((), (), s32[]{:S(2)}) async-start(), calls=%async_computation.9 | async-start | bytes 1949696 | tf_op jit(solution)/shard_map/all_gather | solution.py:83
  455.1 196.8 %reduce-scatter.8.cloned.1.call-start = ((), (), s32[]{:S(2)}) async-start(), calls=%async_computation.10 | async-start | bytes 4874240 | tf_op jit(solution)/shard_map/reduce_scatter | solution.py:84
  540.0 0.7 copy-start.7
  540.0 0.9 copy-start.2
Sparse Core Ops, SparseCore 0:
  10.4 78.4 all-gather.4
  92.2 118.3 all-gather.6
  213.3 74.6 all-gather.8
  290.4 76.8 reduce-scatter.5
  369.9 83.4 reduce-scatter.3
  455.6 79.0 all-gather.10
  540.1 111.7 reduce-scatter.7
